TPU v7x, 32 devices: a whole 2x2x4 slice. The times are simulated.
32 devices in a mesh: layer: 4 (over z), feat: 8 (over y, x, core).
Axes of the slice: x: 2, y: 2, z: 4, core: 2. Of those that a mesh axis runs over, the one named last changes fastest.
Arguments:
- residuals: bfloat16 [4, 64, 4608], P('layer', 'feat'), may hold values from -60 to 60
- enc_weight: bfloat16 [4, 4608, 16384], P('layer', None, 'feat'), may hold values from -0.09375 to 0.09375
- enc_bias: float32 [4, 16384], P('layer', 'feat'), may hold values from -3 to 3
- thresh_levels: int32 [4, 16384], P('layer', 'feat'), may hold values from 2 to 8
- dec_weight: bfloat16 [4, 4, 4608, 16384], P('layer', None, 'feat'), may hold values from -0.046875 to 0.046875
- dec_bias: float32 [4, 4608], P('layer', 'feat'), may hold values from -3 to 3
Outputs:
- recon: bfloat16 [4, 64, 4608], P('layer', None, 'feat')
All inputs are finite; a program needn't handle non-finite values.
Results may differ from a plain program's by a relative error of at most 0.0053.
Values may be sent and summed in bfloat16 or wider, within the bound.
A program may use at most 192 MiB of HBM per device.

v0:
```python
import jax
import jax.numpy as jnp
from jax import lax
from jax.sharding import PartitionSpec as P


def per_device(residuals, enc_weight, enc_bias, thresh_levels, dec_weight, dec_bias):
    layers = dec_weight.shape[1]
    my_layer = lax.axis_index("layer")
    theta = thresh_levels[0].astype(jnp.float32) * 0.125
    keep = (jnp.arange(layers) >= my_layer)[:, None, None]
    resid_float = lax.all_gather(residuals, "feat", axis=1, tiled=True)[0].astype(jnp.float32)
    factor = lax.rsqrt(jnp.mean(resid_float * resid_float, axis=-1, keepdims=True) + 1e-06)
    normed = (resid_float * factor).astype(jnp.bfloat16)
    pre = jnp.dot(normed, enc_weight[0], preferred_element_type=jnp.float32) + enc_bias[0]
    activity = (pre * jnp.clip((pre - theta) / 0.25, 0.0, 1.0)).astype(jnp.bfloat16)
    decoder = dec_weight[0]
    partials = jnp.einsum(
        "rf,edf->erd",
        lax.all_gather(activity, "feat", axis=1, tiled=True),
        decoder,
        preferred_element_type=jnp.float32,
    )
    partials = jnp.where(keep, partials, 0.0)
    total = lax.psum_scatter(partials, "layer", scatter_dimension=0, tiled=True)
    return (total + dec_bias[0]).astype(jnp.bfloat16)


def solution(mesh):
    in_specs = (
        P("layer", "feat", None),
        P("layer", None, "feat"),
        P("layer", "feat"),
        P("layer", "feat"),
        P("layer", None, "feat", None),
        P("layer", "feat"),
    )
    out_specs = P("layer", None, "feat")
    return jax.shard_map(
        per_device, mesh=mesh, in_specs=in_specs, out_specs=out_specs, check_vma=False
    )
```

profile of v0, /device:TPU:0, one launch (start us, length us, event | category | flops | bytes accessed | tf_op | source)
XLA Modules:
  0.0 120.3 jit_solution(15574021523245266452)
XLA Ops:
  6.5 0.0 all-gather.2.cloned.1.call-start
  6.5 11.8 %all_gather.6 = bf16[1,64,4608]{2,1,0:T(8,128)(2,1)S(1)} all-gather(bf16[1,8,4608]{2,1,0:T(8,128)(2,1)} %param.6), channel_id=1, replica_groups=mesh['layer'=4,'feat'=8] {'feat'}, dimensions={1}, use_global_device_ids=true | all-gather | bytes 663552 | tf_op jit(solution)/shard_map/all_gather | solution.py:12
  18.3 0.2 fusion.8
  18.5 0.7 convert_multiply_fusion.2
  19.3 10.6 %multiply_convert_fusion = bf16[64,2048]{1,0:T(8,128)(2,1)} fusion(bf16[1,4608,2048]{2,1,0:T(8,128)(2,1)} %param.7, bf16[1,64,4608]{2,1,0:T(8,128)(2,1)S(1)} %all_gather.6, f32[64]{0:T(128)S(1)} %add_rsqrt_fusion, f32[2048]{0:T(1024)S(1)} %bitcast.30, f32[2048]{0:T(1024)} %bitcast.31), kind=kOutput, calls=%fused_computation.14 | convolution fusion | flops 1209630720 | bytes 19742976 | tf_op jit(solution)/shard_map/dot_general | solution.py:15
  29.9 0.0 all-gather.2.cloned.1.call-update
  29.9 0.0 reduce-scatter.2.cloned.1.call-start
  30.0 0.0 copy-start
  30.0 28.3 %all-gather.2.cloned.1.call-done = bf16[64,16384]{1,0:T(8,128)(2,1)} async-done(((bf16[64,2048]{1,0:T(8,128)(2,1)}), bf16[64,16384]{1,0:T(8,128)(2,1)}) %all-gather.2.cloned.1.call-update) | async-done | bytes 2097168 | tf_op jit(solution)/shard_map/all_gather | solution.py:20
  58.2 31.3 %fusion.15 = f32[4,64,576]{2,1,0:T(8,128)} fusion(bf16[1,4,576,16384]{3,2,1,0:T(8,128)(2,1)} %param.10, bf16[64,16384]{1,0:T(8,128)(2,1)} %all-gather.2.cloned.1.call-done, pred[4]{0:T(512)(128)(4,1)S(1)} %iota_compare_fusion), kind=kOutput, calls=%fused_computation.11 | convolution fusion | flops 4831985664 | bytes 78184448 | tf_op jit(solution)/shard_map/rf,edf->erd/dot_general | solution.py:18
  89.6 0.0 reduce-scatter.2.cloned.1.call-update
  89.6 0.0 copy-done
  89.6 22.3 %reduce-scatter.2.cloned.1.call-done = f32[1,64,576]{2,1,0:T(8,128)} async-done(((f32[4,64,576]{2,1,0:T(8,128)}), f32[1,64,576]{2,1,0:T(8,128)}) %reduce-scatter.2.cloned.1.call-update) | async-done | bytes 147472 | tf_op jit(solution)/shard_map/reduce_scatter | solution.py:25
  111.9 1.6 %add_convert_fusion = bf16[1,64,576]{2,1,0:T(8,128)(2,1)} fusion(f32[1,64,576]{2,1,0:T(8,128)} %reduce-scatter.2.cloned.1.call-done, f32[576]{0:T(1024)S(1)} %reduce.1), kind=kLoop, calls=%fused_computation.15 | loop fusion | flops 73728 | bytes 223488 | tf_op jit(solution)/shard_map/convert_element_type | solution.py:26
  (3 shorter events, 0.0 us)
Async XLA Ops:
  6.5 51.7 %all-gather.2.cloned.1.call-start = ((), (), s32[]{:S(2)}) async-start(), calls=%async_computation.1 | async-start | bytes 2359296 | tf_op jit(solution)/shard_map/all_gather | solution.py:20
  29.9 82.0 %reduce-scatter.2.cloned.1.call-start = ((), (), s32[]{:S(2)}) async-start(), calls=%async_computation.2 | async-start | bytes 819200 | tf_op jit(solution)/shard_map/reduce_scatter | solution.py:25
  30.0 59.6 %copy-start = (f32[1,576]{1,0:T(1,128)S(1)}, f32[1,576]{1,0:T(1,128)}, u32[]{:S(2)}) copy-start(f32[1,576]{1,0:T(1,128)} %param.11) | copy-start | bytes 6916
Sparse Core Ops, SparseCore 0:
  30.0 28.1 all-gather.1
  89.7 22.1 reduce-scatter.1
where the time goes:
time: 121 us; the launch traced here: 120 us
  waiting for transfers between devices  50.6 us (42%)
  matrix products  42 us (35%)
  between operations  13.4 us (11%)
  blocking collectives  11.8 us (10%)
  other arithmetic  2.53 us (2%)
    dot_general x1, matrix products, per_device(): jnp.einsum('rf,edf->erd', lax.all_gather(activity, 'feat', axis=1, tiled=...  31.3 us
    all_gather x1, waiting for transfers between devices, per_device(): lax.all_gather(activity, 'feat', axis=1, tiled=True)  28.3 us
    reduce_scatter x1, waiting for transfers between devices, per_device(): total = lax.psum_scatter(partials, 'layer', scatter_dimension=0, tiled=True)  22.3 us
    all_gather x1, blocking collectives, per_device(): lax.all_gather(residuals, 'feat', axis=1, tiled=True)[0].astype(jnp.float32)  11.8 us
    dot_general x1, matrix products, per_device(): jnp.dot(normed, enc_weight[0], preferred_element_type=jnp.float32)  10.6 us
  transfers between devices with their start and end apart: 2, of which 2 were waited for; matrix products, arithmetic and copies ran while one was open for 0% of the time, Pallas kernels for 0%

commit v1 on v0

--- a/solution.py
+++ b/solution.py
@@ -1,10 +1,18 @@
+import functools
+
 import jax
 import jax.numpy as jnp
 from jax import lax
+from jax.experimental import pallas as pl
+from jax.experimental.pallas import tpu as pltpu
 from jax.sharding import PartitionSpec as P
 
-
-def per_device(residuals, enc_weight, enc_bias, thresh_levels, dec_weight, dec_bias):
+MESH = pl.DeviceIdType.MESH
+VMEM_BYTES = 63 * 2**20
+VMEM_SPARE = 3 * 2**20
+
+
+def plain(residuals, enc_weight, enc_bias, thresh_levels, dec_weight, dec_bias):
     layers = dec_weight.shape[1]
     my_layer = lax.axis_index("layer")
     theta = thresh_levels[0].astype(jnp.float32) * 0.125
@@ -14,11 +22,10 @@
     normed = (resid_float * factor).astype(jnp.bfloat16)
     pre = jnp.dot(normed, enc_weight[0], preferred_element_type=jnp.float32) + enc_bias[0]
     activity = (pre * jnp.clip((pre - theta) / 0.25, 0.0, 1.0)).astype(jnp.bfloat16)
-    decoder = dec_weight[0]
     partials = jnp.einsum(
         "rf,edf->erd",
         lax.all_gather(activity, "feat", axis=1, tiled=True),
-        decoder,
+        dec_weight[0],
         preferred_element_type=jnp.float32,
     )
     partials = jnp.where(keep, partials, 0.0)
@@ -26,7 +33,285 @@
     return (total + dec_bias[0]).astype(jnp.bfloat16)
 
 
+def xor(a, b, size):
+    out, bit = 0, 1
+    while bit < size:
+        x, y = lax.rem(lax.div(a, bit), 2), lax.rem(lax.div(b, bit), 2)
+        out = out + bit * (x + y - 2 * x * y)
+        bit *= 2
+    return out
+
+
+def kernel(
+    layers, n, parts, slots,
+    resid_ref, enc_ref, bias_ref, level_ref, dec_ref, dbias_ref, out_ref,
+    gathered, normed, enc_buf, acts, dec_buf, acc, outbox, inbox,
+    res_send, res_recv, resf_send, resf_recv,
+    act_send, act_recv, actf_send, actf_recv,
+    sum_send, sum_recv, enc_sem, dec_sem,
+):
+    chips = n // 2
+    layer = lax.axis_index("layer")
+    feat = lax.axis_index("feat")
+    chip, core = lax.div(feat, 2), lax.rem(feat, 2)
+    mate = feat + 1 - 2 * core
+    rows = resid_ref.shape[1]
+    width = resid_ref.shape[2]
+    half = width // 2
+    cols = acts.shape[3]
+    dests = layers - layer
+    total = dests * n
+    near = n // 2
+
+    def block_of(place):
+        other = xor(chip, lax.div(place, 2), chips)
+        side = lax.rem(place, 2)
+        return 2 * other + core + side - 2 * core * side
+
+    def partner(k):
+        return mate if k == 0 else 2 * xor(chip, jnp.int32(k), chips) + core
+
+    def step_of(c):
+        early = c < near * dests
+        late = c - near * dests
+        place = jnp.where(early, lax.div(c, dests), near + lax.rem(late, n - near))
+        dest = jnp.where(early, lax.rem(c, dests), lax.div(late, n - near))
+        return place, layers - 1 - dest
+
+    def dec_copy(c):
+        place, dest = step_of(c)
+        size = parts * cols
+        start = pl.multiple_of(block_of(place) * size, size)
+        slot = lax.rem(c, slots)
+        return pltpu.make_async_copy(
+            dec_ref.at[0, dest, :, pl.ds(start, size)], dec_buf.at[slot], dec_sem.at[slot]
+        )
+
+    def enc_copy(i):
+        return pltpu.make_async_copy(
+            enc_ref.at[0, :, pl.ds(pl.multiple_of(i * cols, cols), cols)],
+            enc_buf.at[i], enc_sem.at[i],
+        )
+
+    def remote(src, dst, send, recv, where):
+        return pltpu.make_async_remote_copy(
+            src_ref=src, dst_ref=dst, send_sem=send, recv_sem=recv,
+            device_id=where, device_id_type=MESH,
+        )
+
+    def res_copy(k):
+        return remote(gathered.at[feat], gathered.at[feat], res_send.at[k], res_recv.at[k],
+                      (layer, partner(k)))
+
+    def resf_copy(k):
+        block = partner(k)
+        return remote(gathered.at[block], gathered.at[block], resf_send.at[k], resf_recv.at[k],
+                      (layer, mate))
+
+    def act_copy(k, i):
+        return remote(acts.at[feat, i], acts.at[feat, i], act_send.at[k, i], act_recv.at[k, i],
+                      (layer, partner(k)))
+
+    def actf_copy(k):
+        block = 2 * xor(chip, k, chips) + core
+        return remote(acts.at[block], acts.at[block], actf_send.at[k], actf_recv.at[k],
+                      (layer, mate))
+
+    def sum_copy(dest):
+        return remote(outbox.at[dest], inbox.at[layer], sum_send.at[dest], sum_recv.at[layer],
+                      (dest, feat))
+
+    for i in range(parts):
+        enc_copy(i).start()
+
+    barrier = pltpu.get_barrier_semaphore()
+    for k in range(chips):
+        pl.semaphore_signal(barrier, inc=1, device_id=(layer, partner(k)), device_id_type=MESH)
+    for k in range(1, layers):
+        pl.semaphore_signal(barrier, inc=1, device_id=(lax.rem(layer + k, layers), feat),
+                            device_id_type=MESH)
+
+    x = resid_ref[0].astype(jnp.float32)
+    x = x * lax.rsqrt(jnp.mean(x * x, axis=-1, keepdims=True) + 1e-06)
+    gathered[feat] = jnp.concatenate([x[:, :half], x[:, half:]], axis=0).astype(jnp.bfloat16)
+
+    pl.semaphore_wait(barrier, chips + layers - 1)
+    for k in range(chips - 1, -1, -1):
+        res_copy(k).start()
+    first = min(2, slots)
+
+    def prefetch(c, carry):
+        @pl.when(c < total)
+        def _():
+            dec_copy(c).start()
+        return carry
+
+    lax.fori_loop(0, first, prefetch, 0)
+    acc[...] = jnp.zeros_like(acc)
+    for k in range(1, chips):
+        res_copy(k).wait_recv()
+        resf_copy(k).start()
+    res_copy(0).wait_recv()
+    for k in range(1, chips):
+        resf_copy(k).wait_recv()
+
+    for pair in range(n // 2):
+        low = gathered[2 * pair].astype(jnp.float32)
+        high = gathered[2 * pair + 1].astype(jnp.float32)
+        at = pl.ds(2 * rows * pair, 2 * rows)
+        normed[at, :half] = jnp.concatenate([low[:rows], high[:rows]], axis=0).astype(jnp.bfloat16)
+        normed[at, half:] = jnp.concatenate([low[rows:], high[rows:]], axis=0).astype(jnp.bfloat16)
+
+    each = -(-(slots - first) // parts)
+
+    def encode(i, carry):
+        enc_copy(i).wait()
+        lax.fori_loop(first + i * each, jnp.minimum(first + (i + 1) * each, slots), prefetch, 0)
+        here = pl.ds(pl.multiple_of(i * cols, cols), cols)
+        pre = jnp.dot(normed[...], enc_buf[i], preferred_element_type=jnp.float32)
+        pre = pre + bias_ref[:, here]
+        theta = level_ref[:, here].astype(jnp.float32) * 0.125
+        acts[feat, i] = (pre * jnp.clip((pre - theta) * 4.0, 0.0, 1.0)).astype(jnp.bfloat16)
+        for k in range(chips):
+            act_copy(k, i).start()
+        return carry
+
+    lax.fori_loop(0, parts, encode, 0)
+
+    def arrive(place):
+        k = lax.div(place, 2)
+        direct = jnp.logical_or(place == 1, jnp.logical_and(place > 1, lax.rem(place, 2) == 0))
+
+        @pl.when(direct)
+        def _():
+            for i in range(parts):
+                remote(acts.at[feat, i], acts.at[feat, i], act_send.at[k, i], act_recv.at[k, i],
+                       (layer, mate)).wait_recv()
+
+        @pl.when(jnp.logical_and(direct, place > 1))
+        def _():
+            actf_copy(k).start()
+
+        @pl.when(jnp.logical_and(place > 1, lax.rem(place, 2) == 1))
+        def _():
+            actf_copy(k).wait_recv()
+
+    def decode(c, carry):
+        place, dest = step_of(c)
+
+        @pl.when(dest == layers - 1)
+        def _():
+            arrive(place)
+
+        block = block_of(place)
+        slot = lax.rem(c, slots)
+        dec_copy(c).wait()
+        part = acc[dest]
+        for i in range(parts):
+            part = part + lax.dot_general(
+                dec_buf[slot, :, i * cols:(i + 1) * cols], acts[block, i],
+                (((1,), (1,)), ((), ())), preferred_element_type=jnp.float32,
+            )
+        acc[dest] = part
+
+        @pl.when(c + slots < total)
+        def _():
+            dec_copy(c + slots).start()
+
+        @pl.when(jnp.logical_and(place == n - 1, dest > layer))
+        def _():
+            outbox[dest] = acc[dest].T
+            sum_copy(dest).start()
+
+        return carry
+
+    lax.fori_loop(0, total, decode, 0)
+
+    result = acc[layer].T + dbias_ref[...]
+    outbox[layer] = result
+    for source in range(layers - 1):
+        @pl.when(source < layer)
+        def _():
+            remote(outbox.at[0], inbox.at[source], sum_send.at[0], sum_recv.at[source],
+                   (layer, mate)).wait_recv()
+            outbox[layer] = outbox[layer] + inbox[source]
+    out_ref[0] = outbox[layer].astype(jnp.bfloat16)
+
+    for k in range(chips):
+        res_copy(k).wait_send()
+        for i in range(parts):
+            act_copy(k, i).wait_send()
+    for k in range(1, chips):
+        resf_copy(k).wait_send()
+        actf_copy(jnp.int32(k)).wait_send()
+    for dest in range(1, layers):
+        @pl.when(dest > layer)
+        def _():
+            sum_copy(dest).wait_send()
+
+
+def fused(layers, n, residuals, enc_weight, enc_bias, thresh_levels, dec_weight, dec_bias):
+    rows, width = residuals.shape[1:]
+    features = enc_weight.shape[2]
+    out_rows = dec_weight.shape[2]
+    tokens = rows * n
+    chips = n // 2
+    parts = 4
+    cols = features // parts
+    pad = lambda x: -(-x // 128) * 128
+    fixed = (
+        2 * n * rows * width * 2 + width * features * 2 + n * tokens * features * 2
+        + layers * out_rows * pad(tokens) * 4 + 2 * layers * tokens * pad(out_rows) * 4
+        + rows * width * 2 + 4 * 8 * features * 4 + tokens * pad(out_rows) * 2
+    )
+    slot_bytes = out_rows * features * 2
+    slots = max(1, min(layers * n, (VMEM_BYTES - VMEM_SPARE - fixed) // slot_bytes))
+    dma = pltpu.SemaphoreType.DMA
+    vmem = pl.BlockSpec(memory_space=pltpu.VMEM)
+    hbm = pl.BlockSpec(memory_space=pl.ANY)
+    weights = width * features + layers * out_rows * features * n
+    return pl.pallas_call(
+        functools.partial(kernel, layers, n, parts, slots),
+        out_shape=jax.ShapeDtypeStruct((1, tokens, out_rows), jnp.bfloat16),
+        in_specs=[vmem, hbm, vmem, vmem, hbm, vmem],
+        out_specs=vmem,
+        scratch_shapes=[
+            pltpu.VMEM((n, 2 * rows, width // 2), jnp.bfloat16),
+            pltpu.VMEM((tokens, width), jnp.bfloat16),
+            pltpu.VMEM((parts, width, cols), jnp.bfloat16),
+            pltpu.VMEM((n, parts, tokens, cols), jnp.bfloat16),
+            pltpu.VMEM((slots, out_rows, features), jnp.bfloat16),
+            pltpu.VMEM((layers, out_rows, tokens), jnp.float32),
+            pltpu.VMEM((layers, tokens, out_rows), jnp.float32),
+            pltpu.VMEM((layers, tokens, out_rows), jnp.float32),
+            dma((chips,)), dma((chips,)), dma((chips,)), dma((chips,)),
+            dma((chips, parts)), dma((chips, parts)), dma((chips,)), dma((chips,)),
+            dma((layers,)), dma((layers,)), dma((parts,)), dma((slots,)),
+        ],
+        compiler_params=pltpu.CompilerParams(
+            collective_id=0, has_side_effects=True, vmem_limit_bytes=VMEM_BYTES
+        ),
+        cost_estimate=pl.CostEstimate(
+            flops=2 * tokens * weights, bytes_accessed=2 * weights, transcendentals=0
+        ),
+    )(residuals, enc_weight, enc_bias, thresh_levels, dec_weight, dec_bias)
+
+
 def solution(mesh):
+    layers, n = mesh.shape["layer"], mesh.shape["feat"]
+
+    def per_device(*args):
+        residuals, enc_weight, _, _, dec_weight, _ = args
+        fits = (
+            dec_weight.shape[1] == layers
+            and n >= 4 and n & (n - 1) == 0
+            and residuals.shape[1] % 8 == 0
+            and residuals.shape[2] % 256 == 0
+            and enc_weight.shape[2] % 1024 == 0
+            and dec_weight.shape[2] % 16 == 0
+        )
+        return fused(layers, n, *args) if fits else plain(*args)
+
     in_specs = (
         P("layer", "feat", None),
         P("layer", None, "feat"),

time: 121 us -> 51 us (0.42)
  waiting for transfers between devices: 50.6 us -> 0 us
  Pallas kernels: 0 us -> 48.9 us
  matrix products: 42 us -> 0 us
  between operations: 13.4 us -> 0.01 us
  blocking collectives: 11.8 us -> 0 us
  other arithmetic: 2.53 us -> 0 us
  local copies, waits for them, and re-layouts: 0.01 us -> 1.53 us
    pallas_call x0 -> x1, Pallas kernels: none -> 48.9 us  [fused(): pl.pallas_call(functools.partial(kernel, layers, n, parts, slots), out_sh...]
    dot_general x2 -> x0, matrix products: 42 us -> none  [the longest x1 31.3 us: per_device(): jnp.einsum('rf,edf->erd', lax.all_gather(activity, 'feat', axis=1, tiled=...]
    all_gather x1 -> x0, waiting for transfers between devices: 28.3 us -> none  [per_device(): lax.all_gather(activity, 'feat', axis=1, tiled=True)]
    reduce_scatter x1 -> x0, waiting for transfers between devices: 22.3 us -> none  [per_device(): total = lax.psum_scatter(partials, 'layer', scatter_dimension=0, tiled=True)]
    all_gather x1 -> x0, blocking collectives: 11.8 us -> none  [per_device(): lax.all_gather(residuals, 'feat', axis=1, tiled=True)[0].astype(jnp.float32)]
    convert_element_type x1 -> x0, other arithmetic: 1.56 us -> none  [per_device(): return (total + dec_bias[0]).astype(jnp.bfloat16)]
    unnamed x2 -> x1, local copies, waits for them, and re-layouts: 0.01 us -> 1.53 us
  transfers between devices with their start and end apart: 2 -> 0, of which waited for: 2 -> 0; matrix products, arithmetic and copies ran while one was open for 0% -> 0% of each run, Pallas kernels for 0% -> 0%
where the time goes in v1:
time: 51 us; the launch traced here: 50.4 us
  Pallas kernels  48.9 us (96%)
  local copies, waits for them, and re-layouts  1.53 us (3%)
    pallas_call x1, Pallas kernels, fused(): pl.pallas_call(functools.partial(kernel, layers, n, parts, slots), out_sh...  48.9 us
    unnamed x1, local copies, waits for them, and re-layouts  1.53 us

profile of v1, /device:TPU:0, one launch (start us, length us, event | category | flops | bytes accessed | tf_op | source)
XLA Modules:
  0.0 50.4 jit_solution(1383968337016816237)
XLA Ops:
  0.0 48.9 %shard_map.64 = bf16[1,64,576]{2,1,0:T(8,128)(2,1)} custom-call(bf16[1,8,4608]{2,1,0:T(8,128)(2,1)} %resid_ref.1, bf16[1,4608,2048]{2,1,0:T(8,128)(2,1)} %enc_ref.1, f32[1,2048]{1,0:T(1,128)} %bias_ref.1, s32[1,2048]{1,0:T(1,128)} %level_ref.1, bf16[1,4,576,16384]{3,2,1,0:T(8,128)(2,1)} %dec_ref.1, f32[1,576]{1,0:T(1,128)} %dbias_ref.1), custom_call_target="tpu_custom_call" | custom-call | flops 6039797760 | bytes 94371840 | tf_op jit(solution)/shard_map/pallas_call | solution.py:273
  48.9 1.5 %copy.8 = bf16[1,64,576]{2,1,0:T(8,128)(2,1)} copy(bf16[1,64,576]{2,1,0:T(8,128)(2,1)} %shard_map.64) | data formatting | bytes 147456
